TPU v7x, 128 devices: a whole 4x4x4 slice. The times are simulated.
128 devices in a mesh: pos: 64 (over y, x_hi, z, core), frame: 2 (over x_lo).
Axes of the slice: x: 4 (x_hi: 2, x_lo: 2; x = x_hi * 2 + x_lo), y: 4, z: 4, core: 2. Of those that a mesh axis runs over, the one named last changes fastest.
Arguments:
- tokens: bfloat16 [8, 16, 256, 768], P('frame', None, 'pos'), may hold values from -6 to 6
- modulation: float32 [8, 2, 2, 6, 768], P('frame'), may hold values from -3 to 3
- box_bounds: int32 [8, 6], P('frame'), may hold values from 0 to 16, as said below
- masters: float32 [896, 128, 128], P('pos')
- left_stats: float32 [896, 128, 128], P('pos'), as said below
- right_stats: float32 [896, 128, 128], P('pos'), as said below
- left_roots: float32 [896, 128, 128], P('pos'), as said below
- right_roots: float32 [896, 128, 128], P('pos'), as said below
- owner_slot: int32 [864], replicated, may hold values from 0 to 895, as said below
- cotangent: bfloat16 [8, 16, 256, 768], P('frame', None, 'pos'), may hold values from -6 to 6
Outputs:
- block_output: bfloat16 [8, 16, 256, 768], P('frame', None, 'pos')
- token_grads: bfloat16 [8, 16, 256, 768], P('frame', None, 'pos')
- tile_grads: float32 [896, 128, 128], P('pos')
- new_left: float32 [896, 128, 128], P('pos')
- new_right: float32 [896, 128, 128], P('pos')
- new_masters: float32 [896, 128, 128], P('pos')
Inputs may be any that keep to these rules, and one draw needn't show every extreme that they name: Distinct slots: tile t of the weights is held at slot owner_slot[t]; the other 32 slots hold no tile. For each clip c: box_bounds[c, 0] < box_bounds[c, 1] <= 16, box_bounds[c, 2] < box_bounds[c, 3] <= 16, box_bounds[c, 4] < box_bounds[c, 5] <= 16. `left_stats`: each slot's matrix is symmetric positive definite. `right_stats`: each slot's matrix is symmetric positive definite. `left_roots`: each slot's matrix is symmetric positive definite. `right_roots`: each slot's matrix is symmetric positive definite.
All inputs are finite; a program needn't handle non-finite values.
Results may differ from a plain program's by a relative error of at most 0.015.
Values may be sent and summed in bfloat16 or wider, within the bound.
No kernel may reach another device: no remote copies, remote signals or barrier semaphores. Data moves between devices by JAX's collectives and lax.ppermute only.
A program may use at most 320 MiB of HBM per device.

v0:
```python
import jax
import jax.numpy as jnp
from jax import lax
from jax.sharding import Mesh
from jax.sharding import PartitionSpec as P

D = 768
HEADS = 12
HD = 64
FF = 3072
GRID = 16
BLOCK = 128
POS = ("pos_0", "pos_1", "pos_2", "pos_3")


highest = lax.Precision.HIGHEST
stat_decay = 0.5
learning_rate = 0.7
norm_epsilon = 1e-06


def sent_together(arrays, axis, split_dim, concat_dim, along):
    widths = [a.shape[along] for a in arrays]
    both = jnp.concatenate(arrays, axis=along)
    filled = lax.all_to_all(both, axis, split_axis=split_dim, concat_axis=concat_dim, tiled=True)
    return tuple(jnp.split(filled, [sum(widths[:k]) for k in range(1, len(widths))], axis=along))


def split_up(value, dim, size):
    shape = value.shape
    blocks = value.reshape(*shape[:dim], size, shape[dim] // size, *shape[dim + 1 :])
    return jnp.moveaxis(blocks, dim, 0)


def sum_by_chip(value, chips, core, dim):
    sizes = (lax.axis_size(chips), lax.axis_size(core))
    blocks = split_up(value, dim, sizes[0] * sizes[1])
    inside = blocks.shape[1:]
    blocks = blocks.reshape(*sizes, *inside).swapaxes(0, 1).reshape(-1, *inside)
    blocks = lax.psum_scatter(blocks, core, scatter_dimension=0, tiled=True)
    return lax.psum_scatter(blocks, chips, scatter_dimension=0, tiled=True)[0]


def from_everyone(value, axis):
    size = lax.axis_size(axis)
    return lax.all_to_all(
        jnp.broadcast_to(value[None], (size, *value.shape)), axis, 0, 0, tiled=True
    )


def over_copies(value, axis):
    everything = from_everyone(value, axis)
    return jnp.sum(everything.astype(jnp.float32), axis=0)


def layer_norm(values):
    center = values - jnp.mean(values, axis=-1, keepdims=True)
    spread = jnp.mean(center * center, axis=-1, keepdims=True)
    return center * lax.rsqrt(spread + norm_epsilon)


def modulated(values, scale_part, shift_part):
    return layer_norm(values) * (1.0 + scale_part) + shift_part


def inside(box_bounds, frame_ids, row_ids, col_ids):

    def edge_at(column):
        return box_bounds[:, column][:, None, None]

    return (
        (edge_at(0) <= frame_ids)
        & (frame_ids < edge_at(1))
        & (edge_at(2) <= row_ids)
        & (row_ids < edge_at(3))
        & (edge_at(4) <= col_ids)
        & (col_ids < edge_at(5))
    )


def split_tiles(tile_set):
    layers = []
    offset = 0
    for layer_index in range(2):
        matrices = []
        for row_count, col_count in ((D, 3 * D), (D, D), (D, FF), (FF, D)):
            tile_count = row_count // BLOCK * (col_count // BLOCK)
            matrices.append(
                tile_set[offset : offset + tile_count].reshape(
                    row_count // BLOCK, col_count // BLOCK, BLOCK, BLOCK
                )
            )
            offset = offset + tile_count
        layers.append(matrices)
    return layers


def tiled(values):
    return values.reshape(values.shape[:-1] + (values.shape[-1] // BLOCK, BLOCK))


def untiled(values):
    return values.reshape(values.shape[:-2] + (values.shape[-2] * values.shape[-1],))


def apply_tiles(values, weight_tiles):
    return untiled(
        jnp.einsum(
            "...ia,ijab->...jb", tiled(values), weight_tiles, preferred_element_type=jnp.float32
        )
    )


def apply_back(grads, weight_tiles):
    return untiled(
        jnp.einsum(
            "...jb,ijab->...ia", tiled(grads), weight_tiles, preferred_element_type=jnp.float32
        )
    )


def outer_tiles(values, grads):
    left_rows = tiled(values).reshape(-1, values.shape[-1] // BLOCK, BLOCK)
    right_rows = tiled(grads).reshape(-1, grads.shape[-1] // BLOCK, BLOCK)
    return jnp.einsum("nia,njb->ijab", left_rows, right_rows, preferred_element_type=jnp.float32)


def score_grad(attn_probs, grad_probs):
    inner_sum = jnp.sum(attn_probs * grad_probs, axis=-1, keepdims=True)
    return (attn_probs * (grad_probs - inner_sum)).astype(jnp.bfloat16)


def temporal_forward(normed, qkv_weight, out_weight):
    clip_count, frame_count, patch_count = normed.shape[:3]
    joined = apply_tiles(normed, qkv_weight)

    def heads_of(col_start):
        picked = joined[..., col_start : col_start + D].astype(jnp.bfloat16)
        return picked.reshape(clip_count, frame_count, patch_count, HEADS, HD)

    queries, keyset, valueset = (heads_of(0), heads_of(D), heads_of(2 * D))
    scores = jnp.einsum(
        "cqphe,ckphe->cphqk", queries, keyset, preferred_element_type=jnp.float32
    ) * HD ** (-0.5)
    attn_probs = jax.nn.softmax(scores, axis=-1)
    probs_low = attn_probs.astype(jnp.bfloat16)
    attended = jnp.einsum(
        "cphqk,ckphe->cqphe", probs_low, valueset, preferred_element_type=jnp.float32
    )
    attended = attended.astype(jnp.bfloat16).reshape(clip_count, frame_count, patch_count, D)
    branch = apply_tiles(attended, out_weight)
    return (branch, (normed, queries, keyset, valueset, attn_probs, probs_low, attended))


def temporal_backward(stored, grad_branch, qkv_weight, out_weight):
    normed, queries, keyset, valueset, attn_probs, probs_low, attended = stored
    scaling = HD ** (-0.5)
    pair_count = D // BLOCK
    out_grad = outer_tiles(attended, grad_branch)
    grad_attended = apply_back(grad_branch, out_weight).astype(jnp.bfloat16).reshape(queries.shape)
    grad_probs = jnp.einsum(
        "cqphe,ckphe->cphqk", grad_attended, valueset, preferred_element_type=jnp.float32
    )
    grad_scores = score_grad(attn_probs, grad_probs)
    grad_queries = (
        jnp.einsum("cphqk,ckphe->cqphe", grad_scores, keyset, preferred_element_type=jnp.float32)
        * scaling
    ).astype(jnp.bfloat16)
    grad_keys = (
        jnp.einsum("cphqk,cqphe->ckphe", grad_scores, queries, preferred_element_type=jnp.float32)
        * scaling
    ).astype(jnp.bfloat16)
    grad_values = jnp.einsum(
        "cphqk,cqphe->ckphe", probs_low, grad_attended, preferred_element_type=jnp.float32
    ).astype(jnp.bfloat16)
    token_shape = normed.shape
    grad_pieces = (
        grad_queries.reshape(token_shape),
        grad_keys.reshape(token_shape),
        grad_values.reshape(token_shape),
    )
    qkv_grad = jnp.concatenate([outer_tiles(normed, piece) for piece in grad_pieces], axis=1)
    grad_normed = apply_back(grad_pieces[0], qkv_weight[:, 0:pair_count])
    grad_normed = grad_normed + apply_back(
        grad_pieces[1], qkv_weight[:, pair_count : 2 * pair_count]
    )
    grad_normed = grad_normed + apply_back(
        grad_pieces[2], qkv_weight[:, 2 * pair_count : 3 * pair_count]
    )
    return (grad_normed, qkv_grad, out_grad)


def swapped_forward(normed, qkv_weight, out_weight):
    clip_count, frame_count, patch_count = normed.shape[:3]
    seq_count = clip_count * frame_count
    pair_count = HEADS // 2
    pair_width = 2 * HD
    flat_tiles = normed.reshape(seq_count, patch_count, D // BLOCK, BLOCK)

    def project(group):
        weight_part = qkv_weight[:, group * pair_count : (group + 1) * pair_count]
        projected = jnp.einsum(
            "spia,ijab->sjpb", flat_tiles, weight_part, preferred_element_type=jnp.float32
        )
        return projected.astype(jnp.bfloat16).reshape(
            seq_count * pair_count, patch_count, pair_width
        )

    queries, keyset, valueset = sent_together((project(0), project(1), project(2)), POS, 0, 1, 2)
    item_count, key_total = (queries.shape[0], queries.shape[1])

    def split_pair(values):
        return values.reshape(item_count, key_total, 2, HD)

    queries, keyset, valueset = (split_pair(queries), split_pair(keyset), split_pair(valueset))
    scores = jnp.einsum(
        "iqhe,ikhe->ihqk", queries, keyset, preferred_element_type=jnp.float32
    ) * HD ** (-0.5)
    attn_probs = jax.nn.softmax(scores, axis=-1)
    probs_low = attn_probs.astype(jnp.bfloat16)
    attended = jnp.einsum(
        "ihqk,ikhe->iqhe", probs_low, valueset, preferred_element_type=jnp.float32
    )
    attended = attended.astype(jnp.bfloat16).reshape(item_count, key_total, pair_width)
    returned = lax.all_to_all(attended, POS, split_axis=1, concat_axis=0, tiled=True).reshape(
        seq_count, pair_count, patch_count, pair_width
    )
    branch = jnp.einsum("sjpe,jkeb->spkb", returned, out_weight, preferred_element_type=jnp.float32)
    stored = (flat_tiles, queries, keyset, valueset, attn_probs, probs_low, returned)
    return (branch.reshape(clip_count, frame_count, patch_count, D), stored)


def swapped_backward(stored, grad_branch, qkv_weight, out_weight):
    flat_tiles, queries, keyset, valueset, attn_probs, probs_low, returned = stored
    seq_count, pair_count, patch_count, pair_width = returned.shape
    item_count, key_total = (queries.shape[0], queries.shape[1])
    scaling = HD ** (-0.5)
    grad_flat = grad_branch.reshape(seq_count, patch_count, D // BLOCK, BLOCK)
    out_grad = jnp.einsum(
        "sjpe,spkb->jkeb", returned, grad_flat, preferred_element_type=jnp.float32
    )
    grad_returned = jnp.einsum(
        "spkb,jkeb->sjpe", grad_flat, out_weight, preferred_element_type=jnp.float32
    )
    grad_returned = grad_returned.astype(jnp.bfloat16).reshape(
        seq_count * pair_count, patch_count, pair_width
    )
    grad_attended = lax.all_to_all(
        grad_returned, POS, split_axis=0, concat_axis=1, tiled=True
    ).reshape(item_count, key_total, 2, HD)
    grad_probs = jnp.einsum(
        "iqhe,ikhe->ihqk", grad_attended, valueset, preferred_element_type=jnp.float32
    )
    grad_scores = score_grad(attn_probs, grad_probs)
    grad_queries = (
        jnp.einsum("ihqk,ikhe->iqhe", grad_scores, keyset, preferred_element_type=jnp.float32)
        * scaling
    ).astype(jnp.bfloat16)
    grad_keys = (
        jnp.einsum("ihqk,iqhe->ikhe", grad_scores, queries, preferred_element_type=jnp.float32)
        * scaling
    ).astype(jnp.bfloat16)
    grad_values = jnp.einsum(
        "ihqk,iqhe->ikhe", probs_low, grad_attended, preferred_element_type=jnp.float32
    ).astype(jnp.bfloat16)
    item_shape = (item_count, key_total, pair_width)
    query_back, keys_back, values_back = sent_together(
        (
            grad_queries.reshape(item_shape),
            grad_keys.reshape(item_shape),
            grad_values.reshape(item_shape),
        ),
        POS,
        1,
        0,
        2,
    )

    def unflat(values):
        return values.reshape(seq_count, pair_count, patch_count, pair_width)

    grad_pieces = (unflat(query_back), unflat(keys_back), unflat(values_back))
    qkv_grad = jnp.concatenate(
        [
            jnp.einsum(
                "spia,sjpb->ijab", flat_tiles, grad_piece, preferred_element_type=jnp.float32
            )
            for grad_piece in grad_pieces
        ],
        axis=1,
    )
    grad_normed = jnp.einsum(
        "sjpb,ijab->spia",
        grad_pieces[0],
        qkv_weight[:, 0:pair_count],
        preferred_element_type=jnp.float32,
    )
    grad_normed = grad_normed + jnp.einsum(
        "sjpb,ijab->spia",
        grad_pieces[1],
        qkv_weight[:, pair_count : 2 * pair_count],
        preferred_element_type=jnp.float32,
    )
    grad_normed = grad_normed + jnp.einsum(
        "sjpb,ijab->spia",
        grad_pieces[2],
        qkv_weight[:, 2 * pair_count : 3 * pair_count],
        preferred_element_type=jnp.float32,
    )
    return (grad_normed.reshape(grad_branch.shape), qkv_grad, out_grad)


def block_forward(residual, picked, weights, attend):
    qkv_weight, out_weight, first_weight, second_weight = weights
    normed_wide, norm_pull = jax.vjp(
        lambda values: modulated(values, picked[..., 1, :], picked[..., 0, :]), residual
    )
    normed = normed_wide.astype(jnp.bfloat16)
    branch, stored = attend(normed, qkv_weight, out_weight)
    middle = residual + picked[..., 2, :] * branch
    renormed_wide, second_pull = jax.vjp(
        lambda values: modulated(values, picked[..., 4, :], picked[..., 3, :]), middle
    )
    renormed = renormed_wide.astype(jnp.bfloat16)
    hidden = apply_tiles(renormed, first_weight)
    active_wide, gelu_pull = jax.vjp(jax.nn.gelu, hidden)
    active = active_wide.astype(jnp.bfloat16)
    mlp_out = apply_tiles(active, second_weight)
    output = middle + picked[..., 5, :] * mlp_out
    return (output, (picked, norm_pull, stored, second_pull, renormed, gelu_pull, active))


def block_backward(carried, upstream, weights, attend_back):
    qkv_weight, out_weight, first_weight, second_weight = weights
    picked, norm_pull, stored, second_pull, renormed, gelu_pull, active = carried
    grad_mlp = (picked[..., 5, :] * upstream).astype(jnp.bfloat16)
    second_grad = outer_tiles(active, grad_mlp)
    grad_active = apply_back(grad_mlp, second_weight)
    grad_hidden = gelu_pull(grad_active)[0].astype(jnp.bfloat16)
    first_grad = outer_tiles(renormed, grad_hidden)
    grad_renormed = apply_back(grad_hidden, first_weight)
    grad_middle = upstream + second_pull(grad_renormed)[0]
    grad_branch = (picked[..., 2, :] * grad_middle).astype(jnp.bfloat16)
    grad_normed, qkv_grad, out_grad = attend_back(stored, grad_branch, qkv_weight, out_weight)
    grad_residual = grad_middle + norm_pull(grad_normed)[0]
    return (grad_residual, [qkv_grad, out_grad, first_grad, second_grad])


def local(
    tokens,
    modulation,
    box_bounds,
    masters,
    left_stats,
    right_stats,
    left_roots,
    right_roots,
    owner_slot,
    cotangent,
):
    clip_count, frame_count, patch_count = tokens.shape[:3]
    frame_ids = jnp.arange(frame_count, dtype=jnp.int32)[None, :, None]
    patch_ids = (lax.axis_index(POS) * patch_count + jnp.arange(patch_count, dtype=jnp.int32))[
        None, None, :
    ]
    in_box = inside(box_bounds, frame_ids, patch_ids // GRID, patch_ids % GRID)
    slots_all = lax.all_gather(masters.astype(jnp.bfloat16), POS, axis=0, tiled=True)
    tile_count = owner_slot.shape[0]
    slot_count = slots_all.shape[0]
    layers = split_tiles(jnp.take(slots_all, owner_slot, axis=0))

    def pick_layer(layer_index):
        choose = modulation[:, layer_index]
        return jnp.where(
            in_box[..., None, None], choose[:, 1][:, None, None], choose[:, 0][:, None, None]
        )

    middle, kept_first = block_forward(
        tokens.astype(jnp.float32), pick_layer(0), layers[0], swapped_forward
    )
    mixed_out, kept_second = block_forward(middle, pick_layer(1), layers[1], temporal_forward)
    grad_middle, grads_second = block_backward(
        kept_second, cotangent.astype(jnp.float32), layers[1], temporal_backward
    )
    grad_tokens, grads_first = block_backward(kept_first, grad_middle, layers[0], swapped_backward)
    pieces = [grad_part.reshape(-1, BLOCK, BLOCK) for grad_part in grads_first + grads_second]
    pieces.append(jnp.zeros((1, BLOCK, BLOCK), jnp.float32))
    slot_tile = (
        jnp.full((slot_count,), tile_count, jnp.int32)
        .at[owner_slot]
        .set(jnp.arange(tile_count, dtype=jnp.int32))
    )
    slot_grads = jnp.take(jnp.concatenate(pieces, axis=0), slot_tile, axis=0)
    owned_grads = sum_by_chip(slot_grads, ("pos_0", "pos_1", "pos_2"), "pos_3", 0)
    owned_grads = over_copies(owned_grads.astype(jnp.bfloat16), "frame").astype(jnp.float32)
    product_left = jnp.einsum("sij,skj->sik", owned_grads, owned_grads, precision=highest)
    product_right = jnp.einsum("sji,sjk->sik", owned_grads, owned_grads, precision=highest)
    new_left = stat_decay * left_stats + (1.0 - stat_decay) * product_left
    new_right = stat_decay * right_stats + (1.0 - stat_decay) * product_right
    rotated = jnp.einsum("sij,sjk->sik", owned_grads, right_roots, precision=highest)
    update = jnp.einsum("sij,sjk->sik", left_roots, rotated, precision=highest)
    new_masters = masters - learning_rate * update
    return (
        mixed_out.astype(jnp.bfloat16),
        grad_tokens.astype(jnp.bfloat16),
        owned_grads,
        new_left,
        new_right,
        new_masters,
    )


def solution(mesh):
    split = Mesh(
        mesh.devices.reshape(4, 2, 4, 2, mesh.shape["frame"]),
        ("pos_0", "pos_1", "pos_2", "pos_3", "frame"),
    )
    return jax.shard_map(
        local,
        mesh=split,
        in_specs=(
            P("frame", None, POS, None),
            P("frame", None, None, None, None),
            P("frame", None),
            P(POS, None, None),
            P(POS, None, None),
            P(POS, None, None),
            P(POS, None, None),
            P(POS, None, None),
            P(),
            P("frame", None, POS, None),
        ),
        out_specs=(
            P("frame", None, POS, None),
            P("frame", None, POS, None),
            P(POS, None, None),
            P(POS, None, None),
            P(POS, None, None),
            P(POS, None, None),
        ),
        check_vma=False,
    )
```

profile of v0, /device:TPU:1, one launch (start us, length us, event | category | flops | bytes accessed | tf_op | source)
XLA Modules:
  0.0 1176.8 jit_solution(2909050355645942430)
XLA Ops:
  24.0 136.3 %all-gather.2.cloned.1.call-done = bf16[896,128,128]{2,1,0:T(8,128)(2,1)} async-done(((bf16[14,128,128]{2,1,0:T(8,128)(2,1)}), bf16[896,128,128]{2,1,0:T(8,128)(2,1)}) %all-gather.2.cloned.1.call-update) | async-done | bytes 29360144 | tf_op jit(solution)/shard_map/all_gather | solution.py:367
  160.3 30.9 %gather_fusion = bf16[864,128,128]{2,1,0:T(8,128)(2,1)} fusion(bf16[896,128,128]{2,1,0:T(8,128)(2,1)} %all-gather.2.cloned.1.call-done, s32[1024]{0:T(1024)S(1)} %pad_clamp_fusion.1), kind=kCustom, calls=%fused_computation | custom fusion | bytes 56626560 | tf_op jit(solution)/shard_map/jit(_take)/gather | solution.py:370
  191.2 19.6 %broadcast_select_fusion = bf16[864,128,128]{2,1,0:T(8,128)(2,1)} fusion(bf16[864,128,128]{2,1,0:T(8,128)(2,1)} %gather_fusion, pred[864]{0:T(1024)(128)(4,1)S(1)} %compare_and_fusion.1), kind=kLoop, calls=%fused_computation.6 | loop fusion | flops 14155776 | bytes 56623968 | tf_op jit(solution)/shard_map/jit(_take)/select_n | solution.py:370
  210.8 7.1 fusion.224
  223.9 6.3 all-to-all-start
  231.6 15.8 %fusion.223 = (bf16[144,128,128]{2,1,0:T(8,128)(2,1)}, bf16[144,128,128]{2,1,0:T(8,128)(2,1)}, bf16[144,128,128]{2,1,0:T(8,128)(2,1)}, bf16[144,128,128]{2,1,0:T(8,128)(2,1)}) fusion(bf16[864,128,128]{2,1,0:T(8,128)(2,1)} %broadcast_select_fusion), kind=kLoop, calls=%fused_computation.351 | loop fusion | bytes 37748736 | tf_op jit(solution)/shard_map/slice | solution.py:89
  263.8 7.1 all-to-all-start.1
  276.4 6.6 copy.399
  283.0 6.3 copy.406
  289.3 6.7 copy.384
  296.0 6.4 copy.427
  302.4 6.7 copy.386
  309.1 6.5 copy.425
  316.9 5.8 copy.390
  336.1 5.9 multiply_convert_fusion.2
  441.6 11.0 all-to-all-start.2
  511.0 10.5 all-to-all-start.3
  528.0 9.6 copy.466
  537.6 9.6 copy.471
  547.2 8.0 copy.482
  565.4 9.7 copy.492
  585.5 9.6 copy.497
  602.4 8.4 copy.458
  610.7 6.9 constant_dynamic-update-slice_fusion.7
  619.3 9.2 constant_dynamic-update-slice_fusion.5
  645.0 8.6 constant_dynamic-update-slice_fusion
  654.2 41.5 %gather_fusion.1 = f32[896,128,128]{2,1,0:T(8,128)} fusion(f32[865,128,128]{2,1,0:T(8,128)} %broadcast_dynamic-update-slice_fusion, s32[1024]{0:T(1024)S(1)} %copy-done.81), kind=kCustom, calls=%fused_computation.1 | custom fusion | bytes 117444096 | tf_op jit(solution)/shard_map/jit(_take)/gather | solution.py:393
  695.7 38.8 %copy_select_fusion = f32[32,2,14,128,128]{4,3,2,0,1:T(8,128)} fusion(f32[32,2,14,128,128]{4,3,2,1,0:T(8,128)} %bitcast.698, pred[32,2,14]{2,0,1:T(8,128)(4,1)S(1)} %copy-done.80), kind=kLoop, calls=%fused_computation.5 | loop fusion | flops 14680064 | bytes 117441408 | tf_op jit(solution)/shard_map/jit(_take)/select_n | solution.py:393
  734.5 77.7 %reduce-scatter.3.cloned.1.call-done = f32[32,14,128,128]{3,2,1,0:T(8,128)} async-done(((f32[64,14,128,128]{3,2,1,0:T(8,128)}), f32[32,14,128,128]{3,2,1,0:T(8,128)}) %reduce-scatter.3.cloned.1.call-update) | async-done | bytes 29360144 | tf_op jit(solution)/shard_map/reduce_scatter | solution.py:40
  814.6 6.9 copy.401
  832.6 305.8 %reduce-scatter.5.cloned.1.call-done = f32[1,14,128,128]{3,2,1,0:T(8,128)} async-done(((f32[32,14,128,128]{3,2,1,0:T(8,128)}), f32[1,14,128,128]{3,2,1,0:T(8,128)}) %reduce-scatter.5.cloned.1.call-update) | async-done | bytes 917520 | tf_op jit(solution)/shard_map/reduce_scatter | solution.py:41
  1147.9 9.0 all-to-all-done.4
  (438 shorter events, 306.3 us)
Async XLA Ops:
  7.2 1158.0 %copy-start = (f32[14,128,128]{2,1,0:T(8,128)S(1)}, f32[14,128,128]{2,1,0:T(8,128)}, u32[]{:S(2)}) copy-start(f32[14,128,128]{2,1,0:T(8,128)} %param.17) | copy-start | bytes 2752516
  7.2 153.1 %all-gather.2.cloned.1.call-start = ((), (), s32[]{:S(2)}) async-start(), calls=%async_computation.7 | async-start | bytes 29818880 | tf_op jit(solution)/shard_map/all_gather | solution.py:367
  18.1 203.3 %copy-start.20 = (bf16[64,4,6,128]{3,2,0,1:T(8,128)(2,1)}, bf16[64,4,6,128]{3,2,0,1:T(8,128)(2,1)S(1)}, u32[]{:S(2)}) copy-start(bf16[64,4,6,128]{3,2,0,1:T(8,128)(2,1)S(1)} %reshape.557) | copy-start | bytes 1179652
  223.9 27.0 %all-to-all-start = ((bf16[384,4,384]{2,1,0:T(4,128)(2,1)}), bf16[384,4,384]{2,1,0:T(4,128)(2,1)S(1)}, u32[]{:S(2)}, u32[]{:S(2)}) async-start(bf16[384,4,384]{2,1,0:T(4,128)(2,1)} %pad_maximum_fusion.3), calls=%async_computation | async-start | bytes 2359296 | tf_op jit(solution)/shard_map/all_to_all | solution.py:25
  263.8 67.9 %all-to-all-start.1 = ((bf16[6,256,128]{2,0,1:T(8,128)(2,1)}), bf16[6,256,128]{2,0,1:T(8,128)(2,1)S(1)}, u32[]{:S(2)}, u32[]{:S(2)}) async-start(bf16[6,256,128]{2,0,1:T(8,128)(2,1)} %copy.379), calls=%async_computation.1 | async-start | bytes 1048576 | tf_op jit(solution)/shard_map/all_to_all | solution.py:225
  316.9 9.4 slice-start
  334.3 7.7 slice-start.20
  363.0 7.3 slice-start.16
  367.9 12.0 %copy-start.7 = (f32[4,16,4,768]{3,1,2,0:T(8,128)}, f32[4,16,4,768]{3,1,2,0:T(8,128)S(1)}, u32[]{:S(2)}) copy-start(f32[4,16,4,768]{3,1,2,0:T(8,128)S(1)} %get-tuple-element.90) | copy-start | bytes 2359300
  405.6 19.2 %slice-start.8 = ((s8[4718592]{0:T(1024)(128)(4,1)}), s8[524288]{0:T(1024)(128)(4,1)S(1)}, s32[]{:S(2)}) async-start(s8[4718592]{0:T(1024)(128)(4,1)} %bitcast.717), calls=%async_computation.18 | async-start | bytes 1048576
  424.8 10.0 slice-start.12
  425.2 11.6 copy-start.14
  427.1 7.8 slice-start.13
  441.6 16.1 %copy-start.17 = (bf16[4,16,4,3072]{3,2,1,0:T(4,128)(2,1)S(1)}, bf16[4,16,4,3072]{3,2,1,0:T(4,128)(2,1)}, u32[]{:S(2)}) copy-start(bf16[4,16,4,3072]{3,2,1,0:T(4,128)(2,1)} %copy.468) | copy-start | bytes 4718596
  441.6 44.8 %all-to-all-start.2 = ((bf16[384,4,128]{2,1,0:T(4,128)(2,1)}), bf16[384,4,128]{2,1,0:T(4,128)(2,1)}, u32[]{:S(2)}, u32[]{:S(2)}) async-start(bf16[384,4,128]{2,1,0:T(4,128)(2,1)} %bitcast.157), calls=%async_computation.2 | async-start | bytes 786432 | tf_op jit(solution)/shard_map/all_to_all | solution.py:248
  484.6 9.3 copy-start.84
  511.0 84.2 %all-to-all-start.3 = ((bf16[6,256,384]{2,0,1:T(8,128)(2,1)}), bf16[6,256,384]{2,0,1:T(8,128)(2,1)}, u32[]{:S(2)}, u32[]{:S(2)}) async-start(bf16[6,256,384]{2,0,1:T(8,128)(2,1)} %pad_maximum_fusion.2), calls=%async_computation.3 | async-start | bytes 3145728 | tf_op jit(solution)/shard_map/all_to_all | solution.py:25
  521.5 290.7 %reduce-scatter.3.cloned.1.call-start = ((), (), s32[]{:S(2)}) async-start(), calls=%async_computation.8 | async-start | bytes 88080384 | tf_op jit(solution)/shard_map/reduce_scatter | solution.py:40
  565.4 9.7 copy-start.38
  617.7 10.8 slice-start.2
  619.3 9.2 slice-start.3
  619.3 9.2 slice-start.4
  619.3 13.6 %slice-start.10 = ((s8[7077888]{0:T(1024)(128)(4,1)}), s8[4194304]{0:T(1024)(128)(4,1)S(1)}, s32[]{:S(2)}) async-start(s8[7077888]{0:T(1024)(128)(4,1)} %bitcast.721), calls=%async_computation.20 | async-start | bytes 8388608
  632.8 7.5 slice-start.6
  632.9 7.8 slice-start.7
  645.0 9.2 copy-start.81
  654.2 41.5 %copy-start.80 = (pred[32,2,14]{2,0,1:T(8,128)(4,1)S(1)}, pred[32,2,14]{2,0,1:T(8,128)(4,1)}, u32[]{:S(2)}) copy-start(pred[32,2,14]{2,0,1:T(8,128)(4,1)} %copy.451) | copy-start | bytes 2692
  734.5 403.9 %reduce-scatter.5.cloned.1.call-start = ((), (), s32[]{:S(2)}) async-start(), calls=%async_computation.9 | async-start | bytes 30277632 | tf_op jit(solution)/shard_map/reduce_scatter | solution.py:41
  831.0 314.2 %copy-start.15 = (f32[4,16,4,768]{3,1,2,0:T(8,128)S(1)}, f32[4,16,4,768]{3,1,2,0:T(8,128)}, u32[]{:S(2)}) copy-start(f32[4,16,4,768]{3,1,2,0:T(8,128)} %copy-done.14) | copy-start | bytes 2359300
  831.0 314.2 %copy-start.76 = (f32[4,16,4]{1,2,0:T(4,128)S(1)}, f32[4,16,4]{1,2,0:T(4,128)}, u32[]{:S(2)}) copy-start(f32[4,16,4]{1,2,0:T(4,128)} %copy-done.75) | copy-start | bytes 3076
  1140.7 16.1 %all-to-all-start.4 = ((bf16[2,14,128,128]{3,2,1,0:T(8,128)(2,1)}), bf16[2,14,128,128]{3,2,1,0:T(8,128)(2,1)}, u32[]{:S(2)}, u32[]{:S(2)}) async-start(bf16[2,14,128,128]{3,2,1,0:T(8,128)(2,1)} %broadcast_in_dim.155), calls=%async_computation.6 | async-start | bytes 1835008 | tf_op jit(solution)/shard_map/all_to_all | solution.py:46
  1146.9 11.4 copy-start.64
  (84 other events, 299.9 us)
Sparse Core Ops, SparseCore 0:
  11.9 148.3 all-gather.1
  734.6 77.5 reduce-scatter.2
  814.6 323.6 reduce-scatter.4
where the time goes:
time: 1180 us
  waiting for transfers between devices  532 us (45%)
  local copies, waits for them, and re-layouts  386 us (33%)
  matrix products  108 us (9%)
  other arithmetic  94.5 us (8%)
  starting transfers between devices  39.4 us (3%)
  between operations  15.7 us (1%)
    reduce_scatter x1, waiting for transfers between devices, sum_by_chip(): return lax.psum_scatter(blocks, chips, scatter_dimension=0, tiled=True)[0]  306 us
    all_gather x1, waiting for transfers between devices, local(): lax.all_gather(masters.astype(jnp.bfloat16), POS, axis=0, tiled=True)  136 us
    reduce_scatter x1, waiting for transfers between devices, sum_by_chip(): blocks = lax.psum_scatter(blocks, core, scatter_dimension=0, tiled=True)  77.7 us
    unnamed x231, local copies, waits for them, and re-layouts  61.2 us
    reshape x11, local copies, waits for them, and re-layouts, split_tiles(): tile_set[offset:offset + tile_count]  57.6 us
    gather x1, local copies, waits for them, and re-layouts, local(): slot_grads = jnp.take(jnp.concatenate(pieces, axis=0), slot_tile, axis=0)  41.5 us
    transpose x5, local copies, waits for them, and re-layouts, outer_tiles(): jnp.einsum('nia,njb->ijab', left_rows, right_rows, preferred_element_type...  40.5 us
    select_n x2, other arithmetic, local(): slot_grads = jnp.take(jnp.concatenate(pieces, axis=0), slot_tile, axis=0)  38.8 us
  transfers between devices with their start and end apart: 8, of which 5 were waited for; matrix products, arithmetic and copies ran while one was open for 19% of the time, Pallas kernels for 0%

commit v1 on v0

v1 whole, which is shorter than its diff:
```python
import functools

import jax
import jax.numpy as jnp
from jax import lax
from jax.experimental import pallas as pl
from jax.experimental.pallas import tpu as pltpu
from jax.sharding import Mesh
from jax.sharding import PartitionSpec as P

D = 768
HEADS = 12
HD = 64
FF = 3072
GRID = 16
BLOCK = 128
TOK = 256
CH = 256
POS = ("pos_0", "pos_1", "pos_2", "pos_3")
EVERY = ("pos_0", "pos_1", "pos_2", "pos_3", "frame")

highest = lax.Precision.HIGHEST
stat_decay = 0.5
learning_rate = 0.7
norm_epsilon = 1e-06
f32 = jnp.float32
bf16 = jnp.bfloat16

QKV_AT, OUT_AT, FIRST_AT, SECOND_AT, LAYER_TILES = 0, 108, 144, 288, 432


def dot_nn(a, b):
    return lax.dot_general(a, b, (((1,), (0,)), ((), ())), preferred_element_type=f32)


def dot_nt(a, b):
    return lax.dot_general(a, b, (((1,), (1,)), ((), ())), preferred_element_type=f32)


def dot_tn(a, b):
    return lax.dot_general(a, b, (((0,), (0,)), ((), ())), preferred_element_type=f32)


def side(parts):
    return jnp.concatenate(parts, axis=1)


def norm_parts(values):
    center = values - jnp.mean(values, axis=-1, keepdims=True)
    spread = jnp.mean(center * center, axis=-1, keepdims=True)
    inverse = lax.rsqrt(spread + norm_epsilon)
    return center * inverse, inverse


def norm_back(normal, inverse, grad):
    return inverse * (
        grad
        - jnp.mean(grad, axis=-1, keepdims=True)
        - normal * jnp.mean(grad * normal, axis=-1, keepdims=True)
    )


def picked_row(mod_ref, mask_ref, row):
    clips = mod_ref.shape[0]
    span = TOK // clips
    parts = []
    for clip in range(clips):
        inside_box = jnp.broadcast_to(mask_ref[clip * span : (clip + 1) * span, :], (span, D)) > 0.5
        parts.append(
            jnp.where(
                inside_box,
                jnp.broadcast_to(mod_ref[clip, 1, row : row + 1, :], (span, D)),
                jnp.broadcast_to(mod_ref[clip, 0, row : row + 1, :], (span, D)),
            )
        )
    return parts[0] if clips == 1 else jnp.concatenate(parts, axis=0)


def fetch(slots_ref, owner_ref, held, sem, base, row_tiles, col_tiles):
    step = 6

    def one(turn, carry):
        col = turn // (row_tiles // step)
        first = (turn % (row_tiles // step)) * step
        for k in range(step):
            row = first + k
            pltpu.make_async_copy(
                slots_ref.at[owner_ref[base + row * col_tiles + col]],
                held.at[col, pl.ds(pl.multiple_of(row * BLOCK, BLOCK), BLOCK), :],
                sem,
            ).start()
        return carry

    lax.fori_loop(0, col_tiles * (row_tiles // step), one, 0)


def fetch_done(held, sem):
    pltpu.make_async_copy(held, held, sem).wait()


def forward_part(x, mod_ref, mask_ref, weights, waits, kept, same):
    wq, wo, w1, w2 = weights
    qkv_s, probs_s, attended_s, slope_s, active_s = kept
    lane = lax.broadcasted_iota(jnp.int32, (TOK, BLOCK), 1)
    low_half = lane < HD

    normal, _ = norm_parts(x)
    normed = (normal * (1.0 + picked_row(mod_ref, mask_ref, 1)) + picked_row(mod_ref, mask_ref, 0)).astype(bf16)
    waits[0]()

    def project(j, carry):
        qkv_s[j] = dot_nn(normed, side([wq[2 * j], wq[2 * j + 1]])).astype(bf16)
        return carry

    lax.fori_loop(0, 9, project, 0)

    def attend(c, carry):
        for pair in range(2):
            cols = slice(pair * BLOCK, (pair + 1) * BLOCK)
            q, k, v = qkv_s[c, :, cols], qkv_s[3 + c, :, cols], qkv_s[6 + c, :, cols]
            outs = []
            for e in range(2):
                mine = low_half if e == 0 else jnp.logical_not(low_half)
                scores = dot_nt(k, jnp.where(mine, q, jnp.zeros_like(q))) * HD ** (-0.5)
                if same is not None:
                    scores = jnp.where(same, scores, -jnp.inf)
                grown = jnp.exp(scores - jnp.max(scores, axis=0, keepdims=True))
                probs = (grown * (1.0 / jnp.sum(grown, axis=0, keepdims=True))).astype(bf16)
                probs_s[4 * c + 2 * pair + e] = probs
                outs.append(dot_tn(probs, v))
            attended_s[c, :, cols] = jnp.where(low_half, outs[0], outs[1]).astype(bf16)
        return carry

    lax.fori_loop(0, 3, attend, 0)
    attended = side([attended_s[c] for c in range(3)])
    waits[1]()
    branch = side([dot_nn(attended, side([wo[2 * j], wo[2 * j + 1]])) for j in range(3)])
    middle = x + picked_row(mod_ref, mask_ref, 2) * branch
    normal, _ = norm_parts(middle)
    renormed = (normal * (1.0 + picked_row(mod_ref, mask_ref, 4)) + picked_row(mod_ref, mask_ref, 3)).astype(bf16)
    waits[2]()

    def widen(j, carry):
        u = dot_nn(renormed, side([w1[2 * j], w1[2 * j + 1]]))
        root = (2.0 / 3.141592653589793) ** 0.5
        square = u * u
        bent = jnp.tanh(root * (u + 0.044715 * (square * u)))
        active_s[j] = (0.5 * u * (1.0 + bent)).astype(bf16)
        slope_s[j] = (
            0.5 * (1.0 + bent) + 0.5 * u * (1.0 - bent * bent) * (root * (1.0 + 3 * 0.044715 * square))
        ).astype(bf16)
        return carry

    lax.fori_loop(0, 12, widen, 0)
    active = side([active_s[j] for j in range(12)])
    waits[3]()
    mlp = side([dot_nn(active, side([w2[2 * j], w2[2 * j + 1]])) for j in range(3)])
    return middle, renormed, middle + picked_row(mod_ref, mask_ref, 5) * mlp


def send_tiles(stage, grads_ref, place_ref, sem, at, col_tiles, value, row, col):
    rows, cols = value.shape[0] // BLOCK, value.shape[1] // BLOCK
    for j in range(cols):
        for i in range(rows):
            tile = at + (row + i) * col_tiles + (col + j)
            stage[tile] = value[i * BLOCK : (i + 1) * BLOCK, j * BLOCK : (j + 1) * BLOCK].astype(bf16)
            pltpu.make_async_copy(stage.at[tile], grads_ref.at[place_ref[tile]], sem).start()


def backward_part(x, middle, renormed, upstream, mod_ref, mask_ref, weights, waits, kept, stage, grads_ref, place_ref, sem, acc, wide_s):
    wq, wo, w1, w2 = weights
    qkv_s, probs_s, attended_s, slope_s, active_s = kept
    lane = lax.broadcasted_iota(jnp.int32, (TOK, BLOCK), 1)
    low_half = lane < HD
    send = functools.partial(send_tiles, stage, grads_ref, place_ref, sem)

    grad_mlp = (picked_row(mod_ref, mask_ref, 5) * upstream).astype(bf16)
    renormed_t = renormed.T
    acc[...] = jnp.zeros_like(acc)
    waits[3]()
    waits[2]()

    def narrow(j, carry):
        rows = pl.ds(pl.multiple_of(j * CH, CH), CH)
        grad_active = dot_nt(grad_mlp, side([w2[n, rows, :] for n in range(6)]))
        grad_hidden = (grad_active * slope_s[j].astype(f32)).astype(bf16)
        acc[...] += dot_nt(grad_hidden, side([w1[2 * j], w1[2 * j + 1]]))
        send(FIRST_AT, 24, dot_nn(renormed_t, grad_hidden), 0, 2 * j)
        send(SECOND_AT, 6, dot_tn(active_s[j], grad_mlp), 2 * j, 0)
        return carry

    lax.fori_loop(0, 12, narrow, 0)
    normal, inverse = norm_parts(middle)
    grad_middle = upstream + norm_back(normal, inverse, (1.0 + picked_row(mod_ref, mask_ref, 4)) * acc[...])
    grad_branch = (picked_row(mod_ref, mask_ref, 2) * grad_middle).astype(bf16)
    waits[1]()

    def attend(c, carry):
        rows = pl.ds(pl.multiple_of(c * CH, CH), CH)
        grad_attended = dot_nt(grad_branch, side([wo[n, rows, :] for n in range(6)])).astype(bf16)
        send(OUT_AT, 6, dot_tn(attended_s[c], grad_branch), 2 * c, 0)
        for pair in range(2):
            cols = slice(pair * BLOCK, (pair + 1) * BLOCK)
            q, k, v = qkv_s[c, :, cols], qkv_s[3 + c, :, cols], qkv_s[6 + c, :, cols]
            ga = grad_attended[:, cols]
            grads = []
            for e in range(2):
                mine = low_half if e == 0 else jnp.logical_not(low_half)
                probs_low = probs_s[4 * c + 2 * pair + e]
                probs = probs_low.astype(f32)
                weighed = probs * dot_nt(v, jnp.where(mine, ga, jnp.zeros_like(ga)))
                grad_scores = (weighed - probs * jnp.sum(weighed, axis=0, keepdims=True)).astype(bf16)
                grads.append((dot_tn(grad_scores, k), dot_nn(grad_scores, q), dot_nn(probs_low, ga)))
            for n, scaling in ((0, HD ** (-0.5)), (1, HD ** (-0.5)), (2, 1.0)):
                wide_s[3 * n + c, :, cols] = (
                    jnp.where(low_half, grads[0][n], grads[1][n]) * scaling
                ).astype(bf16)
        return carry

    lax.fori_loop(0, 3, attend, 0)
    normal, inverse = norm_parts(x)
    scale_one = 1.0 + picked_row(mod_ref, mask_ref, 1)
    normed_t = (normal * scale_one + picked_row(mod_ref, mask_ref, 0)).astype(bf16).T
    acc[...] = jnp.zeros_like(acc)
    waits[0]()

    def gather_in(j, carry):
        piece = wide_s[j]
        acc[...] += dot_nt(piece, side([wq[2 * j], wq[2 * j + 1]]))
        send(QKV_AT, 18, dot_nn(normed_t, piece), 0, 2 * j)
        return carry

    lax.fori_loop(0, 9, gather_in, 0)
    normal, inverse = norm_parts(x)
    return grad_middle + norm_back(normal, inverse, scale_one * acc[...])


def same_sequence():
    rows = lax.broadcasted_iota(jnp.int32, (TOK, TOK), 0)
    cols = lax.broadcasted_iota(jnp.int32, (TOK, TOK), 1)
    return jnp.logical_and(rows // 64 == cols // 64, rows % 4 == cols % 4)


WEIGHT_SCRATCH = [
    pltpu.VMEM((18, D, BLOCK), bf16),
    pltpu.VMEM((6, D, BLOCK), bf16),
    pltpu.VMEM((24, D, BLOCK), bf16),
    pltpu.VMEM((6, FF, BLOCK), bf16),
    pltpu.SemaphoreType.DMA((4,)),
]
KEPT = [
    ((9, TOK, CH), bf16),
    ((HEADS, TOK, TOK), bf16),
    ((3, TOK, CH), bf16),
    ((12, TOK, CH), bf16),
    ((12, TOK, CH), bf16),
]
WEIGHT_RUNS = ((QKV_AT, 6, 18), (OUT_AT, 6, 6), (FIRST_AT, 6, 24), (SECOND_AT, 24, 6))


def fetch_all(slots_ref, owner_ref, held, sems, base, order):
    for n in order:
        at, rows, cols = WEIGHT_RUNS[n]
        fetch(slots_ref, owner_ref, held[n], sems.at[n], base + at, rows, cols)
    return [functools.partial(fetch_done, held[n], sems.at[n]) for n in range(4)]


def first_forward(owner_ref, x_ref, mod_ref, mask_ref, slots_ref, middle_ref, out_ref, *rest):
    kept, (wq, wo, w1, w2, sems) = rest[:5], rest[5:]
    weights = (wq, wo, w1, w2)
    waits = fetch_all(slots_ref, owner_ref, weights, sems, 0, (0, 1, 2, 3))
    middle, _, output = forward_part(x_ref[...].astype(f32), mod_ref, mask_ref, weights, waits, kept, None)
    middle_ref[...] = middle
    out_ref[...] = output.astype(bf16)


def second_layer(
    owner_ref, place_ref, x_ref, up_ref, mod_ref, mask_ref, slots_ref, out_ref, grad_ref, grads_ref, *rest
):
    kept, (wq, wo, w1, w2, sems, stage, sem, acc, wide_s) = rest[:5], rest[5:]
    weights = (wq, wo, w1, w2)
    waits = fetch_all(slots_ref, owner_ref, weights, sems, LAYER_TILES, (0, 1, 2, 3))
    x = x_ref[...].astype(f32)
    middle, renormed, output = forward_part(x, mod_ref, mask_ref, weights, waits, kept, same_sequence())
    out_ref[...] = output.astype(bf16)
    nothing = [lambda: None] * 4
    grad = backward_part(
        x, middle, renormed, up_ref[...].astype(f32), mod_ref, mask_ref, weights, nothing, kept,
        stage, grads_ref, place_ref.at[pl.ds(LAYER_TILES, LAYER_TILES)], sem, acc, wide_s,
    )
    grad_ref[...] = grad.astype(bf16)
    pltpu.make_async_copy(stage, grads_ref.at[pl.ds(0, LAYER_TILES)], sem).wait()


def first_backward(
    owner_ref, place_ref, empty_ref, x_ref, middle_ref, up_ref, mod_ref, mask_ref, slots_ref,
    qkv_s, probs_s, attended_s, slope_s, active_s, _, grad_ref, grads_ref,
    wq, wo, w1, w2, sems, stage, sem, acc, wide_s, blank,
):
    weights = (wq, wo, w1, w2)
    waits = fetch_all(slots_ref, owner_ref, weights, sems, 0, (3, 2, 1, 0))
    blank[...] = jnp.zeros_like(blank)
    for k in range(32):
        pltpu.make_async_copy(blank.at[k], grads_ref.at[empty_ref[k]], sem).start()
    x, middle = x_ref[...].astype(f32), middle_ref[...]
    normal, _inverse = norm_parts(middle)
    renormed = (normal * (1.0 + picked_row(mod_ref, mask_ref, 4)) + picked_row(mod_ref, mask_ref, 3)).astype(bf16)
    grad = backward_part(
        x, middle, renormed, up_ref[...].astype(f32), mod_ref, mask_ref, weights, waits,
        (qkv_s, probs_s, attended_s, slope_s, active_s), stage, grads_ref, place_ref, sem, acc, wide_s,
    )
    grad_ref[...] = grad.astype(bf16)
    pltpu.make_async_copy(stage, grads_ref.at[pl.ds(0, LAYER_TILES)], sem).wait()
    pltpu.make_async_copy(blank, grads_ref.at[pl.ds(0, 32)], sem).wait()


SMEM = pl.BlockSpec(memory_space=pltpu.SMEM)
VMEM = pl.BlockSpec(memory_space=pltpu.VMEM)
ANY = pl.BlockSpec(memory_space=pl.ANY)
PARAMS = pltpu.CompilerParams(vmem_limit_bytes=60 * 1024 * 1024)
BACK_SCRATCH = [
    pltpu.VMEM((LAYER_TILES, BLOCK, BLOCK), bf16),
    pltpu.SemaphoreType.DMA,
    pltpu.VMEM((TOK, D), f32),
    pltpu.VMEM((9, TOK, CH), bf16),
]


def run_first_forward(owner, x, mod, mask, slots):
    return pl.pallas_call(
        first_forward,
        name="first_forward",
        out_shape=[jax.ShapeDtypeStruct((TOK, D), f32), jax.ShapeDtypeStruct((TOK, D), bf16)]
        + [jax.ShapeDtypeStruct(s, t) for s, t in KEPT],
        in_specs=[SMEM, VMEM, VMEM, VMEM, ANY],
        out_specs=[VMEM] * 7,
        scratch_shapes=WEIGHT_SCRATCH,
        compiler_params=PARAMS,
    )(owner, x, mod, mask, slots)


def run_second(owner, place, x, up, mod, mask, slots):
    return pl.pallas_call(
        second_layer,
        name="second_layer",
        out_shape=[
            jax.ShapeDtypeStruct((TOK, D), bf16),
            jax.ShapeDtypeStruct((TOK, D), bf16),
            jax.ShapeDtypeStruct(slots.shape, bf16),
        ],
        in_specs=[SMEM, SMEM, VMEM, VMEM, VMEM, VMEM, ANY],
        out_specs=[VMEM, VMEM, ANY],
        scratch_shapes=[pltpu.VMEM(s, t) for s, t in KEPT] + WEIGHT_SCRATCH + BACK_SCRATCH,
        compiler_params=PARAMS,
    )(owner, place, x, up, mod, mask, slots)


def run_first_backward(owner, place, empty, x, middle, up, mod, mask, slots, kept, grads):
    return pl.pallas_call(
        first_backward,
        name="first_backward",
        out_shape=[jax.ShapeDtypeStruct((TOK, D), bf16), jax.ShapeDtypeStruct(grads.shape, bf16)],
        in_specs=[SMEM] * 3 + [VMEM] * 5 + [ANY] + [VMEM] * 5 + [ANY],
        out_specs=[VMEM, ANY],
        scratch_shapes=WEIGHT_SCRATCH + BACK_SCRATCH + [pltpu.VMEM((32, BLOCK, BLOCK), bf16)],
        input_output_aliases={14: 1},
        compiler_params=PARAMS,
    )(owner, place, empty, x, middle, up, mod, mask, slots, *kept, grads)


def inside(box_bounds, frame_ids, patch_ids):
    row_ids, col_ids = patch_ids // GRID, patch_ids % GRID

    def edge(column):
        return box_bounds[..., column]

    return (
        (edge(0) <= frame_ids)
        & (frame_ids < edge(1))
        & (edge(2) <= row_ids)
        & (row_ids < edge(3))
        & (edge(4) <= col_ids)
        & (col_ids < edge(5))
    )


def everyone():
    for y in range(4):
        for xh in range(2):
            for z in range(4):
                for c in range(2):
                    for xl in range(2):
                        yield (y, xh, z, c, xl)


def number(y, xh, z, c, xl):
    return (((y * 2 + xh) * 4 + z) * 2 + c) * 2 + xl


def permute(value, target):
    return lax.ppermute(value, EVERY, [(number(*d), number(*target(*d))) for d in everyone()])


def along(axis, step):
    def target(y, xh, z, c, xl):
        if (axis == 0) == (c == 0):
            return ((y + step) % 4, xh, z, c, xl)
        return (y, xh, (z + step) % 4, c, xl)

    return target


def other_core(y, xh, z, c, xl):
    return (y, xh, z, 1 - c, xl)


def across(y, xh, z, c, xl):
    return (y, 1 - xh, z, c, 1 - xl)


def twin(y, xh, z, c, xl):
    return (y, xh, z, c, 1 - xl)


def added(*values):
    total = values[0].astype(f32)
    for value in values[1:]:
        total = total + value.astype(f32)
    return total.astype(bf16)


def ring_sum(blocks, axis, half):
    ahead = permute(blocks[2][:half], along(axis, 1))
    behind = permute(blocks[2][half:], along(axis, -1))
    up = jnp.concatenate([added(blocks[1][:half], ahead), blocks[1][half:]], axis=0)
    down = jnp.concatenate([blocks[3][:half], added(blocks[3][half:], behind)], axis=0)
    ahead = permute(up, along(axis, 1))
    behind = permute(down, along(axis, -1))
    return added(blocks[0], ahead, behind)


def reduce_tiles(grads, core):
    mine, others = grads[: 448], grads[448:]

    def joined(r):
        piece = slice(r * 112, (r + 1) * 112)
        return added(mine[piece], permute(others[piece], other_core))

    blocks = {r: joined(r) for r in (2, 1, 3, 0)}
    total = ring_sum(blocks, 0, 56)
    blocks = {r: total[r * 28 : (r + 1) * 28] for r in range(4)}
    total = ring_sum(blocks, 1, 14)
    part = added(total[:14], permute(total[14:], across))
    whole = part.astype(f32) + permute(part, twin).astype(f32)
    by_core = whole.reshape(2, 7, BLOCK, BLOCK)
    own = lax.dynamic_index_in_dim(by_core, core, 0, keepdims=False)
    given = lax.dynamic_index_in_dim(by_core, 1 - core, 0, keepdims=False)
    got = permute(given, other_core)
    return jnp.where(core == 0, jnp.concatenate([own, got], axis=0), jnp.concatenate([got, own], axis=0))


def place_of(slots, y, xh, z, core):
    owner, k = slots // 14, slots % 14
    owner_y, owner_xh, owner_z, owner_c = owner // 16, owner // 8 % 2, owner // 2 % 4, owner % 2
    handler = k // 7
    ahead_y, ahead_z = (owner_y - y) % 4, (owner_z - z) % 4
    first = jnp.where(handler == 0, ahead_y, ahead_z)
    second = jnp.where(handler == 0, ahead_z, ahead_y)
    place = (handler + core) % 2
    for extent, index in ((4, first), (4, second), (2, (owner_xh + xh) % 2), (2, owner_c), (7, k % 7)):
        place = place * extent + index
    return place.astype(jnp.int32)


def local(
    tokens,
    modulation,
    box_bounds,
    masters,
    left_stats,
    right_stats,
    left_roots,
    right_roots,
    owner_slot,
    cotangent,
):
    y, xh, z, core = (lax.axis_index(a) for a in POS)
    mine = lax.axis_index(POS)
    slots_all = lax.all_gather(masters.astype(bf16), POS, axis=0, tiled=True)

    def to_frames(value):
        return lax.all_to_all(value.reshape(64, 4, D), POS, 0, 0, tiled=True).reshape(TOK, D)

    clip, frame = mine // 16, mine % 16
    tokens_here = to_frames(tokens)
    mod_first = lax.dynamic_slice_in_dim(modulation[:, 0], clip, 1, 0)
    bounds_here = lax.dynamic_index_in_dim(box_bounds, clip, 0, keepdims=True)
    mask_first = inside(bounds_here, frame, jnp.arange(TOK, dtype=jnp.int32))
    mask_first = mask_first.astype(f32).reshape(TOK, 1)
    ids = jnp.arange(TOK, dtype=jnp.int32)
    bounds_rows = jnp.repeat(box_bounds, 64, axis=0)
    mask_second = inside(bounds_rows, ids // 4 % 16, mine * 4 + ids % 4).astype(f32).reshape(TOK, 1)

    place = place_of(owner_slot, y, xh, z, core)
    free = jnp.ones((896,), jnp.int32).at[owner_slot].set(0)
    empty = place_of(jnp.nonzero(free, size=32)[0].astype(jnp.int32), y, xh, z, core)

    middle, passed, *kept = run_first_forward(owner_slot, tokens_here, mod_first, mask_first, slots_all)
    here = to_frames(passed)
    block_output, grad_here, grads = run_second(
        owner_slot, place, here, cotangent.reshape(TOK, D), modulation[:, 1], mask_second, slots_all
    )
    upstream = to_frames(grad_here)
    token_grads, grads = run_first_backward(
        owner_slot, place, empty, tokens_here, middle, upstream, mod_first, mask_first, slots_all, kept, grads
    )
    token_grads = to_frames(token_grads)
    owned_grads = reduce_tiles(grads, core)

    product_left = jnp.einsum("sij,skj->sik", owned_grads, owned_grads, precision=highest)
    product_right = jnp.einsum("sji,sjk->sik", owned_grads, owned_grads, precision=highest)
    new_left = stat_decay * left_stats + (1.0 - stat_decay) * product_left
    new_right = stat_decay * right_stats + (1.0 - stat_decay) * product_right
    rotated = jnp.einsum("sij,sjk->sik", owned_grads, right_roots, precision=highest)
    update = jnp.einsum("sij,sjk->sik", left_roots, rotated, precision=highest)
    new_masters = masters - learning_rate * update
    return (
        block_output.reshape(tokens.shape),
        token_grads.reshape(tokens.shape),
        owned_grads,
        new_left,
        new_right,
        new_masters,
    )


def solution(mesh):
    split = Mesh(
        mesh.devices.reshape(4, 2, 4, 2, mesh.shape["frame"]),
        ("pos_0", "pos_1", "pos_2", "pos_3", "frame"),
    )
    return jax.shard_map(
        local,
        mesh=split,
        in_specs=(
            P("frame", None, POS, None),
            P("frame", None, None, None, None),
            P("frame", None),
            P(POS, None, None),
            P(POS, None, None),
            P(POS, None, None),
            P(POS, None, None),
            P(POS, None, None),
            P(),
            P("frame", None, POS, None),
        ),
        out_specs=(
            P("frame", None, POS, None),
            P("frame", None, POS, None),
            P(POS, None, None),
            P(POS, None, None),
            P(POS, None, None),
            P(POS, None, None),
        ),
        check_vma=False,
    )
```

time: 1180 us -> 494 us (0.42)
  local copies, waits for them, and re-layouts: 386 us -> 33 us
  waiting for transfers between devices: 532 us -> 259 us
  matrix products: 108 us -> 10.8 us
  Pallas kernels: 0 us -> 84.3 us
  other arithmetic: 94.5 us -> 34.6 us
    reduce_scatter x2 -> x0, waiting for transfers between devices: 383 us -> none  [the longest x1 306 us: sum_by_chip(): return lax.psum_scatter(blocks, chips, scatter_dimension=0, tiled=True)[0]]
    ppermute x0 -> x15, waiting for transfers between devices: none -> 112 us  [permute(): lax.ppermute(value, EVERY, [(number(*d), number(*target(*d))) for d in ev...]
    dot_general x44 -> x0, matrix products: 91.3 us -> none  [the longest x8 23.4 us: outer_tiles(): jnp.einsum('nia,njb->ijab', left_rows, right_rows, preferred_element_type...]
    pallas_call x0 -> x3, Pallas kernels: none -> 84.3 us  [the longest x1 37.6 us: run_second(): pl.pallas_call(second_layer, name='second_layer', out_shape=[jax.ShapeDty...]
    gather x2 -> x0, local copies, waits for them, and re-layouts: 72.4 us -> none  [the longest x1 41.5 us: local(): slot_grads = jnp.take(jnp.concatenate(pieces, axis=0), slot_tile, axis=0)]
    reshape x24 -> x8, local copies, waits for them, and re-layouts: 80.3 us -> 9.79 us  [the longest x3 4.52 us: to_frames(): value.reshape(64, 4, D)]
    select_n x6 -> x3, other arithmetic: 61.7 us -> 1.9 us  [the longest x1 1.25 us: reduce_tiles(): jnp.where(core == 0, jnp.concatenate([own, got], axis=0), jnp.concatenate...]
    unnamed x231 -> x24, local copies, waits for them, and re-layouts: 61.2 us -> 5.94 us
  transfers between devices with their start and end apart: 8 -> 20, of which waited for: 5 -> 14; matrix products, arithmetic and copies ran while one was open for 19% -> 6% of each run, Pallas kernels for 0% -> 0%
where the time goes in v1:
time: 494 us; the launch traced here: 487 us
  waiting for transfers between devices  259 us (52%)
  Pallas kernels  84.3 us (17%)
  starting transfers between devices  48.9 us (10%)
  other arithmetic  34.6 us (7%)
  local copies, waits for them, and re-layouts  33 us (7%)
  between operations  16 us (3%)
  matrix products  10.8 us (2%)
    all_gather x1, waiting for transfers between devices, local(): slots_all = lax.all_gather(masters.astype(bf16), POS, axis=0, tiled=True)  121 us
    ppermute x15, waiting for transfers between devices, permute(): lax.ppermute(value, EVERY, [(number(*d), number(*target(*d))) for d in ev...  112 us
    pallas_call x1, Pallas kernels, run_second(): pl.pallas_call(second_layer, name='second_layer', out_shape=[jax.ShapeDty...  37.6 us
    pallas_call x1, Pallas kernels, run_first_backward(): pl.pallas_call(first_backward, name='first_backward', out_shape=[jax.Shap...  29.3 us
    all_to_all x4, starting transfers between devices, to_frames(): lax.all_to_all(value.reshape(64, 4, D), POS, 0, 0, tiled=True)  28.5 us
    all_to_all x4, waiting for transfers between devices, to_frames(): lax.all_to_all(value.reshape(64, 4, D), POS, 0, 0, tiled=True)  25.3 us
    ppermute x15, starting transfers between devices, permute(): lax.ppermute(value, EVERY, [(number(*d), number(*target(*d))) for d in ev...  20.3 us
    pallas_call x1, Pallas kernels, run_first_forward(): pl.pallas_call(first_forward, name='first_forward', out_shape=[jax.ShapeD...  17.4 us
  transfers between devices with their start and end apart: 20, of which 14 were waited for; matrix products, arithmetic and copies ran while one was open for 6% of the time, Pallas kernels for 0%

profile of v1, /device:TPU:1, one launch (start us, length us, event | category | flops | bytes accessed | tf_op | source)
XLA Modules:
  0.0 486.7 jit_solution(15283260776691325956)
XLA Ops:
  9.4 12.5 %all-to-all-start = ((bf16[64,4,768]{2,1,0:T(4,128)(2,1)}), bf16[64,4,768]{2,1,0:T(4,128)(2,1)S(1)}, u32[]{:S(2)}, u32[]{:S(2)}) async-start(bf16[64,4,768]{2,1,0:T(4,128)(2,1)} %bitcast.48), calls=%async_computation | async-start | bytes 786432 | tf_op jit(solution)/shard_map/all_to_all | solution.py:492
  28.4 5.3 %scatter_custom_fusion = s32[896]{0:T(1024)S(1)} fusion(s32[864]{0:T(1024)S(1)} %get-tuple-element.75, s32[864]{0:T(1024)S(1)} %jit_remainder_.2, s32[]{:T(128)} %constant.303.clone.1), kind=kCustom, calls=%fused_computation.169 | custom fusion | bytes 3588 | tf_op jit(solution)/shard_map/scatter | solution.py:505
  34.8 3.3 fusion.27.mask_ref
  38.9 121.5 %all-gather.2.cloned.1.call-done.slots_ref = bf16[896,128,128]{2,1,0:T(8,128)(2,1)} async-done(((bf16[14,128,128]{2,1,0:T(8,128)(2,1)}), bf16[896,128,128]{2,1,0:T(8,128)(2,1)}) %all-gather.2.cloned.1.call-update) | async-done | bytes 29360144 | tf_op jit(solution)/shard_map/all_gather | solution.py:489
  160.4 17.4 %first_forward.1 = (f32[256,768]{1,0:T(8,128)}, bf16[256,768]{1,0:T(8,128)(2,1)}, bf16[9,256,256]{2,1,0:T(8,128)(2,1)}, bf16[12,256,256]{2,1,0:T(8,128)(2,1)}, b...) custom-call(s32[864]{0:T(1024)} %owner_ref.5, ...), custom_call_target="tpu_custom_call" | custom-call | tf_op jit(solution)/shard_map/first_forward/pallas_call | solution.py:330
  179.6 6.3 %all-to-all-start.1 = ((bf16[64,4,768]{2,1,0:T(4,128)(2,1)}), bf16[64,4,768]{2,1,0:T(4,128)(2,1)S(1)}, u32[]{:S(2)}, u32[]{:S(2)}) async-start(bf16[64,4,768]{2,1,0:T(4,128)(2,1)} %reshape.338), calls=%async_computation.1 | async-start | bytes 786432 | tf_op jit(solution)/shard_map/all_to_all | solution.py:492
  186.9 11.5 %all-to-all-done.1 = bf16[64,4,768]{2,1,0:T(4,128)(2,1)S(1)} async-done(((bf16[64,4,768]{2,1,0:T(4,128)(2,1)}), bf16[64,4,768]{2,1,0:T(4,128)(2,1)S(1)}, u32[]{:S(2)}, u32[]{:S(2)}) %all-to-all-start.1) | async-done | bytes 393248 | tf_op jit(solution)/shard_map/all_to_all | solution.py:492
  199.3 37.6 %second_layer.1 = (bf16[256,768]{1,0:T(8,128)(2,1)}, bf16[256,768]{1,0:T(8,128)(2,1)}, bf16[896,128,128]{2,1,0:T(8,128)(2,1)}) custom-call(s32[864]{0:T(1024)} %owner_ref.5, s32[864]{0:T(1024)} %get-tuple-element.76.place_ref, bf16[256,768]{1,0:T(8,128)(2,1)} %reshape.339.x_ref, bf16[256,768]{1,0:T(8,128)(2,1)} %reshape.340.up_ref, ...), custom_call_target="tpu_custom_call" | custom-call | tf_op jit(solution)/shard_map/second_layer/pallas_call | solution.py:343
  238.7 4.6 all-to-all-start.2
  243.3 7.6 %scatter_custom_fusion.1 = s32[32]{0:T(128)S(1)} fusion(s32[896]{0:T(1024)S(1)} %fusion.63, s32[896]{0:T(1024)S(1)} %broadcast.455, s32[]{:T(128)} %constant.302.clone.1), kind=kCustom, calls=%fused_computation.213 | custom fusion | flops 896 | bytes 132 | tf_op jit(solution)/shard_map/scatter-add | solution.py:506
  252.4 3.6 all-to-all-done.2
  256.8 29.3 %first_backward.1 = (bf16[256,768]{1,0:T(8,128)(2,1)}, bf16[896,128,128]{2,1,0:T(8,128)(2,1)}) custom-call(s32[864]{0:T(1024)} %owner_ref.5, s32[864]{0:T(1024)} %get-tuple-element.76.place_ref, s32[32]{0:T(128)} %fusion.68.empty_ref, bf16[256,768]{1,0:T(8,128)(2,1)} %reshape.337.x_ref, ...), custom_call_target="tpu_custom_call", output_to_operand_aliasing={{1}: (14, {})} | custom-call | tf_op jit(solution)/shard_map/first_backward/pallas_call | solution.py:359
  286.1 6.9 %fusion.82 = (bf16[112,128,128]{2,1,0:T(8,128)(2,1)S(1)}, bf16[112,128,128]{2,1,0:T(8,128)(2,1)S(1)}, bf16[112,128,128]{2,1,0:T(8,128)(2,1)S(1)}, bf16[112,128,128]{2,1,0:T(8,128)(2,1)S(1)}) fusion(bf16[896,128,128]{2,1,0:T(8,128)(2,1)} %get-tuple-element.29), kind=kLoop, calls=%fused_computation.215 | loop fusion | bytes 29360128 | tf_op jit(solution)/shard_map/slice | solution.py:447
  294.0 5.7 %collective-permute-done.1 = bf16[112,128,128]{2,1,0:T(8,128)(2,1)S(1)} collective-permute-done((bf16[112,128,128]{2,1,0:T(8,128)(2,1)S(1)}, bf16[112,128,128]{2,1,0:T(8,128)(2,1)S(1)}, u32[]{:S(2)}, u32[]{:S(2)}) %collective-permute-start.1) | collective-permute-done | bytes 3670048 | tf_op jit(solution)/shard_map/ppermute | solution.py:401
  299.6 10.4 %collective-permute-done.5 = bf16[112,128,128]{2,1,0:T(8,128)(2,1)S(1)} collective-permute-done((bf16[112,128,128]{2,1,0:T(8,128)(2,1)S(1)}, bf16[112,128,128]{2,1,0:T(8,128)(2,1)S(1)}, u32[]{:S(2)}, u32[]{:S(2)}) %collective-permute-start.5) | collective-permute-done | bytes 3670048 | tf_op jit(solution)/shard_map/ppermute | solution.py:401
  311.8 8.8 %add_convert_fusion.3 = (bf16[112,128,128]{2,1,0:T(8,128)(2,1)S(1)}, bf16[112,128,128]{2,1,0:T(8,128)(2,1)S(1)}, bf16[112,128,128]{2,1,0:T(8,128)(2,1)S(1)}) fusion(bf16[112,128,128]{2,1,0:T(8,128)(2,1)S(1)} %collective-permute-done.1, bf16[896,128,128]{2,1,0:T(8,128)(2,1)} %get-tuple-element.29, bf16[112,128,128]{2,1,0:T(8,128)(2,1)} %copy-done.3, ...), kind=kLoop, calls=%fused_computation.5 | loop fusion | flops 22020096 | bytes 33030144 | tf_op jit(solution)/shard_map/convert_element_type | solution.py:429
  324.3 19.2 %collective-permute-done.6 = bf16[56,128,128]{2,1,0:T(8,128)(2,1)S(1)} collective-permute-done((bf16[56,128,128]{2,1,0:T(8,128)(2,1)S(1)}, bf16[56,128,128]{2,1,0:T(8,128)(2,1)S(1)}, u32[]{:S(2)}, u32[]{:S(2)}) %collective-permute-start.6) | collective-permute-done | bytes 1835040 | tf_op jit(solution)/shard_map/ppermute | solution.py:401
  347.5 39.1 %collective-permute-done.7 = bf16[112,128,128]{2,1,0:T(8,128)(2,1)S(1)} collective-permute-done((bf16[112,128,128]{2,1,0:T(8,128)(2,1)S(1)}, bf16[112,128,128]{2,1,0:T(8,128)(2,1)S(1)}, u32[]{:S(2)}, u32[]{:S(2)}) %collective-permute-start.7) | collective-permute-done | bytes 3670048 | tf_op jit(solution)/shard_map/ppermute | solution.py:401
  386.6 4.1 collective-permute-done.4
  390.8 4.4 add_convert_fusion
  395.4 2.7 collective-permute-start.10
  398.0 6.2 %collective-permute-done.8 = bf16[14,128,128]{2,1,0:T(8,128)(2,1)S(1)} collective-permute-done((bf16[14,128,128]{2,1,0:T(8,128)(2,1)S(1)}, bf16[14,128,128]{2,1,0:T(8,128)(2,1)S(1)}, u32[]{:S(2)}, u32[]{:S(2)}) %collective-permute-start.8) | collective-permute-done | bytes 458784 | tf_op jit(solution)/shard_map/ppermute | solution.py:401
  404.6 2.4 collective-permute-start.11
  407.2 10.2 %collective-permute-done.11 = bf16[28,128,128]{2,1,0:T(8,128)(2,1)S(1)} collective-permute-done((bf16[28,128,128]{2,1,0:T(8,128)(2,1)S(1)}, bf16[28,128,128]{2,1,0:T(8,128)(2,1)S(1)}, u32[]{:S(2)}, u32[]{:S(2)}) %collective-permute-start.11) | collective-permute-done | bytes 917536 | tf_op jit(solution)/shard_map/ppermute | solution.py:401
  417.4 3.6 collective-permute-done.9
  423.3 6.9 %collective-permute-done.12 = bf16[14,128,128]{2,1,0:T(8,128)(2,1)S(1)} collective-permute-done((bf16[14,128,128]{2,1,0:T(8,128)(2,1)S(1)}, bf16[14,128,128]{2,1,0:T(8,128)(2,1)S(1)}, u32[]{:S(2)}, u32[]{:S(2)}) %collective-permute-start.12) | collective-permute-done | bytes 458784 | tf_op jit(solution)/shard_map/ppermute | solution.py:401
  430.4 7.3 %collective-permute-done.13 = bf16[14,128,128]{2,1,0:T(8,128)(2,1)S(1)} collective-permute-done((bf16[14,128,128]{2,1,0:T(8,128)(2,1)S(1)}, bf16[14,128,128]{2,1,0:T(8,128)(2,1)S(1)}, u32[]{:S(2)}, u32[]{:S(2)}) %collective-permute-start.13) | collective-permute-done | bytes 458784 | tf_op jit(solution)/shard_map/ppermute | solution.py:401
  438.6 7.4 %collective-permute-start.14 = (f32[7,128,128]{2,1,0:T(8,128)}, f32[7,128,128]{2,1,0:T(8,128)}, u32[]{:S(2)}, u32[]{:S(2)}) collective-permute-start(f32[7,128,128]{2,1,0:T(8,128)} %get-tuple-element.72), channel_id=1, source_target_pairs={{0,2},{1,3},{2,0},{3,1},{4,6},{5,7},{6,4},{7,5},{8,10},{9,11},{10,... | collective-permute-start | bytes 1376264 | tf_op jit(solution)/shard_map/ppermute | solution.py:401
  446.9 5.2 %all-to-all-start.3 = ((bf16[64,4,768]{2,1,0:T(4,128)(2,1)}), bf16[64,4,768]{2,1,0:T(4,128)(2,1)}, u32[]{:S(2)}, u32[]{:S(2)}) async-start(bf16[64,4,768]{2,1,0:T(4,128)(2,1)} %reshape.348), calls=%async_computation.3 | async-start | bytes 786432 | tf_op jit(solution)/shard_map/all_to_all | solution.py:492
  454.3 10.2 %all-to-all-done.3 = bf16[64,4,768]{2,1,0:T(4,128)(2,1)} async-done(((bf16[64,4,768]{2,1,0:T(4,128)(2,1)}), bf16[64,4,768]{2,1,0:T(4,128)(2,1)}, u32[]{:S(2)}, u32[]{:S(2)}) %all-to-all-start.3) | async-done | bytes 393248 | tf_op jit(solution)/shard_map/all_to_all | solution.py:492
  465.8 4.5 fusion.3
  470.3 2.6 fusion.2
  (94 shorter events, 42.9 us)
Async XLA Ops:
  7.2 465.7 %copy-start = (f32[14,128,128]{2,1,0:T(8,128)S(1)}, f32[14,128,128]{2,1,0:T(8,128)}, u32[]{:S(2)}) copy-start(f32[14,128,128]{2,1,0:T(8,128)} %param.17) | copy-start | bytes 2752516
  7.2 19.0 %copy-start.6 = (bf16[4,16,4,768]{3,2,1,0:T(4,128)(2,1)S(1)}, bf16[4,16,4,768]{3,2,1,0:T(4,128)(2,1)}, u32[]{:S(2)}) copy-start(bf16[4,16,4,768]{3,2,1,0:T(4,128)(2,1)} %param.19) | copy-start | bytes 1179652
  7.2 20.6 %copy-start.8 = (s32[864]{0:T(1024)S(1)}, s32[864]{0:T(1024)}, u32[]{:S(2)}) copy-start(s32[864]{0:T(1024)} %owner_ref.5) | copy-start | bytes 10372
  7.2 153.2 %all-gather.2.cloned.1.call-start = ((), (), s32[]{:S(2)}) async-start(), calls=%async_computation.4 | async-start | bytes 29818880 | tf_op jit(solution)/shard_map/all_gather | solution.py:489
  9.4 28.7 %all-to-all-start = ((bf16[64,4,768]{2,1,0:T(4,128)(2,1)}), bf16[64,4,768]{2,1,0:T(4,128)(2,1)S(1)}, u32[]{:S(2)}, u32[]{:S(2)}) async-start(bf16[64,4,768]{2,1,0:T(4,128)(2,1)} %bitcast.48), calls=%async_computation | async-start | bytes 786432 | tf_op jit(solution)/shard_map/all_to_all | solution.py:492
  160.4 25.6 %copy-start.9 = (s32[4,6]{1,0:T(4,128)S(1)}, s32[4,6]{1,0:T(4,128)}, u32[]{:S(2)}) copy-start(s32[4,6]{1,0:T(4,128)} %param.12) | copy-start | bytes 292
  179.6 18.8 %all-to-all-start.1 = ((bf16[64,4,768]{2,1,0:T(4,128)(2,1)}), bf16[64,4,768]{2,1,0:T(4,128)(2,1)S(1)}, u32[]{:S(2)}, u32[]{:S(2)}) async-start(bf16[64,4,768]{2,1,0:T(4,128)(2,1)} %reshape.338), calls=%async_computation.1 | async-start | bytes 786432 | tf_op jit(solution)/shard_map/all_to_all | solution.py:492
  238.7 17.2 %all-to-all-start.2 = ((bf16[64,4,768]{2,1,0:T(4,128)(2,1)}), bf16[64,4,768]{2,1,0:T(4,128)(2,1)S(1)}, u32[]{:S(2)}, u32[]{:S(2)}) async-start(bf16[64,4,768]{2,1,0:T(4,128)(2,1)} %reshape.346), calls=%async_computation.2 | async-start | bytes 786432 | tf_op jit(solution)/shard_map/all_to_all | solution.py:492
  293.0 6.7 %collective-permute-start.1 = (bf16[112,128,128]{2,1,0:T(8,128)(2,1)S(1)}, bf16[112,128,128]{2,1,0:T(8,128)(2,1)S(1)}, u32[]{:S(2)}, u32[]{:S(2)}) collective-permute-start(bf16[112,128,128]{2,1,0:T(8,128)(2,1)S(1)} %get-tuple-element.59), channel_id=1, source_target_pairs={{0,2},{1,3},{2,0},{3,1},{4,6},{5,7},{6,4},{7,5},{8,10},{9,11},{10,... | collective-permute-start | bytes 11010056 | tf_op jit(solution)/shard_map/ppermute | solution.py:401
  293.5 16.5 %collective-permute-start.5 = (bf16[112,128,128]{2,1,0:T(8,128)(2,1)S(1)}, bf16[112,128,128]{2,1,0:T(8,128)(2,1)S(1)}, u32[]{:S(2)}, u32[]{:S(2)}) collective-permute-start(bf16[112,128,128]{2,1,0:T(8,128)(2,1)S(1)} %get-tuple-element.57), channel_id=1, source_target_pairs={{0,2},{1,3},{2,0},{3,1},{4,6},{5,7},{6,4},{7,5},{8,10},{9,11},{10,... | collective-permute-start | bytes 11010056 | tf_op jit(solution)/shard_map/ppermute | solution.py:401
  293.6 18.2 %collective-permute-start.2 = (bf16[112,128,128]{2,1,0:T(8,128)(2,1)S(1)}, bf16[112,128,128]{2,1,0:T(8,128)(2,1)}, u32[]{:S(2)}, u32[]{:S(2)}) collective-permute-start(bf16[112,128,128]{2,1,0:T(8,128)(2,1)S(1)} %get-tuple-element.58), channel_id=1, source_target_pairs={{0,2},{1,3},{2,0},{3,1},{4,6},{5,7},{6,4},{7,5},{8,10},{9,11},{10,... | collective-permute-start | bytes 11010056 | tf_op jit(solution)/shard_map/ppermute | solution.py:401
  310.0 1.8 copy-start.3
  321.1 22.4 %collective-permute-start.6 = (bf16[56,128,128]{2,1,0:T(8,128)(2,1)S(1)}, bf16[56,128,128]{2,1,0:T(8,128)(2,1)S(1)}, u32[]{:S(2)}, u32[]{:S(2)}) collective-permute-start(bf16[56,128,128]{2,1,0:T(8,128)(2,1)S(1)} %get-tuple-element.70), channel_id=1, source_target_pairs={{0,96},{1,97},{2,14},{3,15},{4,100},{5,101},{6,2},{7,3},{8,104},{9... | collective-permute-start | bytes 5505032 | tf_op jit(solution)/shard_map/ppermute | solution.py:401
  321.8 24.7 %collective-permute-start.3 = (bf16[56,128,128]{2,1,0:T(8,128)(2,1)S(1)}, bf16[56,128,128]{2,1,0:T(8,128)(2,1)S(1)}, u32[]{:S(2)}, u32[]{:S(2)}) collective-permute-start(bf16[56,128,128]{2,1,0:T(8,128)(2,1)S(1)} %get-tuple-element.69), channel_id=1, source_target_pairs={{0,32},{1,33},{2,6},{3,7},{4,36},{5,37},{6,10},{7,11},{8,40},{9,41... | collective-permute-start | bytes 5505032 | tf_op jit(solution)/shard_map/ppermute | solution.py:401
  322.6 24.9 %collective-permute-start = (bf16[112,128,128]{2,1,0:T(8,128)(2,1)S(1)}, bf16[112,128,128]{2,1,0:T(8,128)(2,1)S(1)}, u32[]{:S(2)}, u32[]{:S(2)}) collective-permute-start(bf16[112,128,128]{2,1,0:T(8,128)(2,1)S(1)} %get-tuple-element.56), channel_id=1, source_target_pairs={{0,2},{1,3},{2,0},{3,1},{4,6},{5,7},{6,4},{7,5},{8,10},{9,11},{10,... | collective-permute-start | bytes 11010056 | tf_op jit(solution)/shard_map/ppermute | solution.py:401
  344.5 42.1 %collective-permute-start.7 = (bf16[112,128,128]{2,1,0:T(8,128)(2,1)S(1)}, bf16[112,128,128]{2,1,0:T(8,128)(2,1)S(1)}, u32[]{:S(2)}, u32[]{:S(2)}) collective-permute-start(bf16[112,128,128]{2,1,0:T(8,128)(2,1)S(1)} %pad_maximum_fusion.1), channel_id=1, source_target_pairs={{0,96},{1,97},{2,14},{3,15},{4,100},{5,101},{6,2},{7,3},{8,104},{9... | collective-permute-start | bytes 11010056 | tf_op jit(solution)/shard_map/ppermute | solution.py:401
  347.4 43.3 %collective-permute-start.4 = (bf16[112,128,128]{2,1,0:T(8,128)(2,1)S(1)}, bf16[112,128,128]{2,1,0:T(8,128)(2,1)S(1)}, u32[]{:S(2)}, u32[]{:S(2)}) collective-permute-start(bf16[112,128,128]{2,1,0:T(8,128)(2,1)S(1)} %pad_maximum_fusion), channel_id=1, source_target_pairs={{0,32},{1,33},{2,6},{3,7},{4,36},{5,37},{6,10},{7,11},{8,40},{9,41... | collective-permute-start | bytes 11010056 | tf_op jit(solution)/shard_map/ppermute | solution.py:401
  395.3 8.9 %collective-permute-start.8 = (bf16[14,128,128]{2,1,0:T(8,128)(2,1)S(1)}, bf16[14,128,128]{2,1,0:T(8,128)(2,1)S(1)}, u32[]{:S(2)}, u32[]{:S(2)}) collective-permute-start(bf16[14,128,128]{2,1,0:T(8,128)(2,1)S(1)} %get-tuple-element.65), channel_id=1, source_target_pairs={{0,4},{1,5},{2,34},{3,35},{4,8},{5,9},{6,38},{7,39},{8,12},{9,13},... | collective-permute-start | bytes 1376264 | tf_op jit(solution)/shard_map/ppermute | solution.py:401
  395.4 8.8 %collective-permute-start.10 = (bf16[14,128,128]{2,1,0:T(8,128)(2,1)S(1)}, bf16[14,128,128]{2,1,0:T(8,128)(2,1)S(1)}, u32[]{:S(2)}, u32[]{:S(2)}) collective-permute-start(bf16[14,128,128]{2,1,0:T(8,128)(2,1)S(1)} %get-tuple-element.66), channel_id=1, source_target_pairs={{0,12},{1,13},{2,98},{3,99},{4,0},{5,1},{6,102},{7,103},{8,4},{9,5... | collective-permute-start | bytes 1376264 | tf_op jit(solution)/shard_map/ppermute | solution.py:401
  404.6 12.8 %collective-permute-start.11 = (bf16[28,128,128]{2,1,0:T(8,128)(2,1)S(1)}, bf16[28,128,128]{2,1,0:T(8,128)(2,1)S(1)}, u32[]{:S(2)}, u32[]{:S(2)}) collective-permute-start(bf16[28,128,128]{2,1,0:T(8,128)(2,1)S(1)} %pad_maximum_fusion.3), channel_id=1, source_target_pairs={{0,12},{1,13},{2,98},{3,99},{4,0},{5,1},{6,102},{7,103},{8,4},{9,5... | collective-permute-start | bytes 2752520 | tf_op jit(solution)/shard_map/ppermute | solution.py:401
  407.2 13.8 %collective-permute-start.9 = (bf16[28,128,128]{2,1,0:T(8,128)(2,1)S(1)}, bf16[28,128,128]{2,1,0:T(8,128)(2,1)S(1)}, u32[]{:S(2)}, u32[]{:S(2)}) collective-permute-start(bf16[28,128,128]{2,1,0:T(8,128)(2,1)S(1)} %pad_maximum_fusion.2), channel_id=1, source_target_pairs={{0,4},{1,5},{2,34},{3,35},{4,8},{5,9},{6,38},{7,39},{8,12},{9,13},... | collective-permute-start | bytes 2752520 | tf_op jit(solution)/shard_map/ppermute | solution.py:401
  421.4 24.6 %copy-start.7 = (bf16[256,768]{1,0:T(8,128)(2,1)S(1)}, bf16[256,768]{1,0:T(8,128)(2,1)}, u32[]{:S(2)}) copy-start(bf16[256,768]{1,0:T(8,128)(2,1)} %get-tuple-element.28) | copy-start | bytes 1179652
  421.4 30.6 %copy-start.2 = (f32[14,128,128]{2,1,0:T(8,128)S(1)}, f32[14,128,128]{2,1,0:T(8,128)}, u32[]{:S(2)}) copy-start(f32[14,128,128]{2,1,0:T(8,128)} %param.13) | copy-start | bytes 2752516
  421.5 8.6 %collective-permute-start.12 = (bf16[14,128,128]{2,1,0:T(8,128)(2,1)S(1)}, bf16[14,128,128]{2,1,0:T(8,128)(2,1)S(1)}, u32[]{:S(2)}, u32[]{:S(2)}) collective-permute-start(bf16[14,128,128]{2,1,0:T(8,128)(2,1)S(1)} %slice.196), channel_id=1, source_target_pairs={{0,17},{1,16},{2,19},{3,18},{4,21},{5,20},{6,23},{7,22},{8,25},{9,... | collective-permute-start | bytes 1376264 | tf_op jit(solution)/shard_map/ppermute | solution.py:401
  430.3 7.4 %collective-permute-start.13 = (bf16[14,128,128]{2,1,0:T(8,128)(2,1)S(1)}, bf16[14,128,128]{2,1,0:T(8,128)(2,1)S(1)}, u32[]{:S(2)}, u32[]{:S(2)}) collective-permute-start(bf16[14,128,128]{2,1,0:T(8,128)(2,1)S(1)} %add_convert_fusion.8), channel_id=1, source_target_pairs={{0,1},{1,0},{2,3},{3,2},{4,5},{5,4},{6,7},{7,6},{8,9},{9,8},{10,11... | collective-permute-start | bytes 1376264 | tf_op jit(solution)/shard_map/ppermute | solution.py:401
  438.6 25.9 %collective-permute-start.14 = (f32[7,128,128]{2,1,0:T(8,128)}, f32[7,128,128]{2,1,0:T(8,128)}, u32[]{:S(2)}, u32[]{:S(2)}) collective-permute-start(f32[7,128,128]{2,1,0:T(8,128)} %get-tuple-element.72), channel_id=1, source_target_pairs={{0,2},{1,3},{2,0},{3,1},{4,6},{5,7},{6,4},{7,5},{8,10},{9,11},{10,... | collective-permute-start | bytes 1376264 | tf_op jit(solution)/shard_map/ppermute | solution.py:401
  446.9 17.7 %all-to-all-start.3 = ((bf16[64,4,768]{2,1,0:T(4,128)(2,1)}), bf16[64,4,768]{2,1,0:T(4,128)(2,1)}, u32[]{:S(2)}, u32[]{:S(2)}) async-start(bf16[64,4,768]{2,1,0:T(4,128)(2,1)} %reshape.348), calls=%async_computation.3 | async-start | bytes 786432 | tf_op jit(solution)/shard_map/all_to_all | solution.py:492
  452.4 17.9 %copy-start.4 = (f32[14,128,128]{2,1,0:T(8,128)S(1)}, f32[14,128,128]{2,1,0:T(8,128)}, u32[]{:S(2)}) copy-start(f32[14,128,128]{2,1,0:T(8,128)} %param.15) | copy-start | bytes 2752516
  465.8 7.1 %copy-start.1 = (f32[14,128,128]{2,1,0:T(8,128)}, f32[14,128,128]{2,1,0:T(8,128)S(1)}, u32[]{:S(2)}) copy-start(f32[14,128,128]{2,1,0:T(8,128)S(1)} %maximum_select_fusion) | copy-start | bytes 2752516
  470.3 4.3 copy-start.5
Sparse Core Ops, SparseCore 0:
  11.9 148.4 all-gather.1
